TPU v7x, 32 devices: a whole 2x2x4 slice. The times are simulated.
32 devices in a mesh: dom: 2 (over core), help: 16 (over z, y, x).
Axes of the slice: x: 2, y: 2, z: 4, core: 2. Of those that a mesh axis runs over, the one named last changes fastest.
Arguments:
- displacement: float32 [3, 4, 64, 16], P(None, 'dom', 'help'), may hold values from -3 to 3
- history: float32 [4, 64, 16, 7, 4096], P('dom', 'help'), may hold values from -1.05 to 1.05, as said below
- stored_stiffness: float32 [4, 64, 16, 6, 6], P('dom', 'help'), may hold values from -2.5 to 2.5
- phases: int32 [16, 256], replicated, may hold values from 0 to 1
- yield_order: int32 [2, 16, 128], P('dom', 'help'), may hold values from 0 to 127, each once within a row
- yield_count: int32 [2, 16], P('dom', 'help'), may hold values from 1 to 128, 256 in all within a row
Outputs:
- nodal_force: float32 [3, 4, 64, 16], P(None, 'dom', 'help')
- point_stress: float32 [4, 64, 16, 6], P('dom', 'help')
Inputs may be any that keep to these rules, and one draw needn't show every extreme that they name: `history`: components 0 to 5 are eigenstrain, component 6 is hardening and lies in 0 to 1. `yield_count`: the counts of the 16 devices that share a dom index sum to 256.
All inputs are finite; a program needn't handle non-finite values.
Results may differ from a plain program's by a relative error of at most 0.0001.
Values sent between devices are 32-bit elements; how exact they have to be, the bound alone decides.
A program may use at most 256 MiB of HBM per device.

v0:
```python
import math

import jax
import jax.numpy as jnp
import numpy as np
from jax import lax
from jax.sharding import PartitionSpec as P

SWEEPS = 3
HMEAN = 16


root_half = math.sqrt(0.5)
root_two = math.sqrt(2.0)
lam_ref = 1.5
mu_ref = 2.0
coupling = (lam_ref + mu_ref) / (mu_ref * (lam_ref + 2.0 * mu_ref))
highest = lax.Precision.HIGHEST
iso_stiffness = np.array(
    [
        [
            (
                (lam_ref + 2.0 * mu_ref if row_id < 3 else 2.0 * mu_ref)
                if row_id == col_id
                else lam_ref if row_id < 3 and col_id < 3 else 0.0
            )
            for col_id in range(6)
        ]
        for row_id in range(6)
    ],
    dtype=np.float32,
)


def shifted(block, axis, distance):
    devices = range(lax.axis_size(axis))
    route = [(i - distance, i) for i in devices if i - distance in devices]
    return lax.ppermute(block, axis, route)


def strain_map(extended):
    diff_x = extended[:, 1:] - extended[:, :-1]
    grad_x = 0.25 * (
        diff_x[:, :, :-1, :-1]
        + diff_x[:, :, 1:, :-1]
        + diff_x[:, :, :-1, 1:]
        + diff_x[:, :, 1:, 1:]
    )
    diff_y = extended[:, :, 1:] - extended[:, :, :-1]
    grad_y = 0.25 * (
        diff_y[:, :-1, :, :-1]
        + diff_y[:, 1:, :, :-1]
        + diff_y[:, :-1, :, 1:]
        + diff_y[:, 1:, :, 1:]
    )
    diff_z = extended[:, :, :, 1:] - extended[:, :, :, :-1]
    grad_z = 0.25 * (
        diff_z[:, :-1, :-1] + diff_z[:, 1:, :-1] + diff_z[:, :-1, 1:] + diff_z[:, 1:, 1:]
    )
    return jnp.stack(
        [
            grad_x[0],
            grad_y[1],
            grad_z[2],
            root_half * (grad_z[1] + grad_y[2]),
            root_half * (grad_z[0] + grad_x[2]),
            root_half * (grad_y[0] + grad_x[1]),
        ]
    )


def phase_maps(phases):
    is_hard = (phases == 1).astype(jnp.float32)
    return (1.0 + is_hard, 1.0 + 2.0 * is_hard, 0.4 + 0.4 * is_hard)


def direction_table(edge_len):
    wave_index = jnp.arange(edge_len, dtype=jnp.int32)
    signed = jnp.where(wave_index < edge_len // 2, wave_index, wave_index - edge_len).astype(
        jnp.float32
    )
    flat_index = jnp.arange(edge_len * edge_len, dtype=jnp.int32)
    first_dir = jnp.broadcast_to(signed[:, None], (edge_len, edge_len * edge_len))
    second_dir = jnp.broadcast_to(
        signed[flat_index // edge_len][None, :], (edge_len, edge_len * edge_len)
    )
    third_dir = jnp.broadcast_to(
        signed[flat_index % edge_len][None, :], (edge_len, edge_len * edge_len)
    )
    square = first_dir * first_dir + second_dir * second_dir + third_dir * third_dir
    inverse_len = jnp.where(square > 0, lax.rsqrt(jnp.maximum(square, 1.0)), 0.0)
    return jnp.stack([first_dir * inverse_len, second_dir * inverse_len, third_dir * inverse_len])


def transform_tables(edge_len):
    wave_index = jnp.arange(edge_len, dtype=jnp.int32)
    angle_one = (
        2.0
        * math.pi
        / edge_len
        * (wave_index[:, None] * wave_index[None, :] % edge_len).astype(jnp.float32)
    )
    flat_index = jnp.arange(edge_len * edge_len, dtype=jnp.int32)
    high_part = flat_index // edge_len
    low_part = flat_index % edge_len
    products = (
        high_part[:, None] * high_part[None, :] + low_part[:, None] * low_part[None, :]
    ) % edge_len
    angle_two = 2.0 * math.pi / edge_len * products.astype(jnp.float32)
    return (jnp.cos(angle_one), jnp.sin(angle_one), jnp.cos(angle_two), jnp.sin(angle_two))


def forward(field_in, tables):
    cos_one, sin_one, cos_two, sin_two = tables
    re_plane = jnp.einsum("bcax,xk->bcak", field_in, cos_two, precision=highest)
    im_plane = -jnp.einsum("bcax,xk->bcak", field_in, sin_two, precision=highest)
    real_out = jnp.einsum("ak,bcax->bckx", cos_one, re_plane, precision=highest) + jnp.einsum(
        "ak,bcax->bckx", sin_one, im_plane, precision=highest
    )
    imag_out = jnp.einsum("ak,bcax->bckx", cos_one, im_plane, precision=highest) - jnp.einsum(
        "ak,bcax->bckx", sin_one, re_plane, precision=highest
    )
    return (real_out, imag_out)


def inverse(real_in, imag_in, tables):
    cos_one, sin_one, cos_two, sin_two = tables
    re_axis = jnp.einsum("ak,bckx->bcax", cos_one, real_in, precision=highest) - jnp.einsum(
        "ak,bckx->bcax", sin_one, imag_in, precision=highest
    )
    im_axis = jnp.einsum("ak,bckx->bcax", sin_one, real_in, precision=highest) + jnp.einsum(
        "ak,bckx->bcax", cos_one, imag_in, precision=highest
    )
    plane = jnp.einsum("bcax,xk->bcak", re_axis, cos_two, precision=highest) - jnp.einsum(
        "bcax,xk->bcak", im_axis, sin_two, precision=highest
    )
    voxels = cos_one.shape[0] * cos_two.shape[0]
    return plane / voxels


def green_apply(tensor_in, directions):
    normals = (directions[0], directions[1], directions[2])
    tensor_yz = tensor_in[..., 3, :, :] * root_half
    tensor_xz = tensor_in[..., 4, :, :] * root_half
    tensor_xy = tensor_in[..., 5, :, :] * root_half
    traction = (
        tensor_in[..., 0, :, :] * normals[0] + tensor_xy * normals[1] + tensor_xz * normals[2],
        tensor_xy * normals[0] + tensor_in[..., 1, :, :] * normals[1] + tensor_yz * normals[2],
        tensor_xz * normals[0] + tensor_yz * normals[1] + tensor_in[..., 2, :, :] * normals[2],
    )
    normal_part = normals[0] * traction[0] + normals[1] * traction[1] + normals[2] * traction[2]

    def entry(first_idx, second_idx):
        return (
            0.5
            / mu_ref
            * (
                normals[first_idx] * traction[second_idx]
                + normals[second_idx] * traction[first_idx]
            )
            - coupling * normal_part * normals[first_idx] * normals[second_idx]
        )

    return jnp.stack(
        [
            entry(0, 0),
            entry(1, 1),
            entry(2, 2),
            root_two * entry(1, 2),
            root_two * entry(0, 2),
            root_two * entry(0, 1),
        ],
        axis=-3,
    )


def stress_law(strain, states, maps):
    lame_mod, shear_mod, strength = maps
    elastic = strain - states[..., :6, :, :]
    trace_sum = elastic[..., 0, :, :] + elastic[..., 1, :, :] + elastic[..., 2, :, :]
    third_part = trace_sum / 3.0
    deviator = [
        elastic[..., 0, :, :] - third_part,
        elastic[..., 1, :, :] - third_part,
        elastic[..., 2, :, :] - third_part,
        elastic[..., 3, :, :],
        elastic[..., 4, :, :],
        elastic[..., 5, :, :],
    ]
    dev_square = sum((part * part for part in deviator))
    yield_limit = strength * (1.0 + states[..., 6, :, :])
    ratio = 2.0 * shear_mod / yield_limit
    factor = lax.rsqrt(1.0 + ratio * ratio * dev_square)
    bulk_mod = lame_mod + 2.0 * shear_mod / 3.0
    outputs = []
    for index in range(6):
        value = 2.0 * shear_mod * factor * deviator[index]
        if index < 3:
            value = value + bulk_mod * trace_sum
        outputs.append(value)
    return jnp.stack(outputs, axis=-3)


def reference_part(strain):
    trace_sum = strain[..., 0, :, :] + strain[..., 1, :, :] + strain[..., 2, :, :]
    volume_part = jnp.stack(
        [trace_sum, trace_sum, trace_sum] + [jnp.zeros_like(trace_sum)] * 3, axis=-3
    )
    return lam_ref * volume_part + 2.0 * mu_ref * strain


def homogenize(strains, states, maps, directions, tables):
    count_in = strains.shape[0]
    edge_len = states.shape[2]
    macro_strain = strains[:, :, None, None]
    current = jnp.broadcast_to(macro_strain, (count_in, 6, edge_len, states.shape[3]))
    for iteration in range(SWEEPS):
        polarization = stress_law(current, states, maps) - reference_part(current)
        real_part, imag_part = forward(polarization, tables)
        real_part = green_apply(real_part, directions)
        imag_part = green_apply(imag_part, directions)
        current = macro_strain - inverse(real_part, imag_part, tables)
    final_stress = stress_law(current, states, maps)
    return jnp.mean(final_stress, axis=(2, 3))


def local(displacement, history, stored_stiffness, phases, yield_order, yield_count):
    elems_x = displacement.shape[1]
    elems_y = displacement.shape[2]
    elems_z = displacement.shape[3]
    points = elems_x * elems_y * elems_z
    edge_len = phases.shape[0]
    helpers = lax.axis_size("help")
    slot_count = (points + helpers - 1) // helpers
    states = history.reshape(points, 7, edge_len, edge_len * edge_len)
    yield_list = yield_order.reshape(points)
    live_count = yield_count.reshape(())
    maps = phase_maps(phases)
    directions = direction_table(edge_len)
    tables = transform_tables(edge_len)
    counts = lax.all_gather(yield_count, "help", axis=1, tiled=True).reshape(helpers)
    starts = jnp.cumsum(counts) - counts
    helper_index = lax.axis_index("help")
    helper_ids = jnp.arange(helpers, dtype=jnp.int32)
    own_start = jnp.sum(jnp.where(helper_ids == helper_index, starts, 0))
    slot_index = jnp.arange(slot_count, dtype=jnp.int32)
    item_index = (helper_ids[:, None] - own_start) % helpers + slot_index[None, :] * helpers
    valid_mask = item_index < live_count
    safe_index = jnp.where(valid_mask, item_index, 0)
    point_index = yield_list[safe_index]
    send_states = jnp.where(valid_mask[:, :, None, None, None], states[point_index], 0.0)
    upper_row = shifted(displacement[:, :1], "dom", -1)
    extended = jnp.concatenate([displacement, upper_row], axis=1)
    upper_column = shifted(extended[:, :, :1], "help", -1)
    extended = jnp.concatenate([extended, upper_column], axis=2)
    extended = jnp.pad(extended, ((0, 0), (0, 0), (0, 0), (0, 1)))
    strain, pullback = jax.vjp(strain_map, extended)
    strain_pts = jnp.transpose(strain, (1, 2, 3, 0)).reshape(points, 6)
    stiffness = stored_stiffness.reshape(points, 6, 6) + jnp.asarray(
        iso_stiffness, dtype=stored_stiffness.dtype
    )
    elastic = jnp.einsum("pij,pj->pi", stiffness, strain_pts, precision=highest)
    point_ids = jnp.arange(points, dtype=jnp.int32)
    send_strain = jnp.where(valid_mask[:, :, None], strain_pts[point_index], 0.0)
    got_states, got_strain = (
        lax.all_to_all(send_states, "help", split_axis=0, concat_axis=0, tiled=True),
        lax.all_to_all(send_strain, "help", split_axis=0, concat_axis=0, tiled=True),
    )
    rank_index = jnp.arange(HMEAN, dtype=jnp.int32) * helpers + helper_index
    source = jnp.sum((starts[None, :] <= rank_index[:, None]).astype(jnp.int32), axis=1) - 1
    source_start = jnp.sum(
        jnp.where(helper_ids[None, :] == source[:, None], starts[None, :], 0), axis=1
    )
    flat_slot = source * slot_count + (rank_index - source_start) // helpers
    work_states = got_states.reshape(helpers * slot_count, 7, edge_len, edge_len * edge_len)[
        flat_slot
    ]
    work_strain = got_strain.reshape(helpers * slot_count, 6)[flat_slot]
    result = homogenize(work_strain, work_states, maps, directions, tables)
    spread = (
        flat_slot[None, :] == jnp.arange(helpers * slot_count, dtype=jnp.int32)[:, None]
    ).astype(jnp.float32)
    returning = jnp.dot(spread, result, precision=highest).reshape(helpers, slot_count, 6)
    returned = lax.all_to_all(returning, "help", split_axis=0, concat_axis=0, tiled=True).reshape(
        helpers * slot_count, 6
    )
    matches = (point_index.reshape(-1)[None, :] == point_ids[:, None]) & valid_mask.reshape(-1)[
        None, :
    ]
    yielded = jnp.dot(matches.astype(jnp.float32), returned, precision=highest)
    yield_flag = jnp.any(matches, axis=1)
    stress_pts = jnp.where(yield_flag[:, None], yielded, elastic)
    stress_field = jnp.transpose(stress_pts.reshape(elems_x, elems_y, elems_z, 6), (3, 0, 1, 2))
    (contrib,) = pullback(stress_field)
    contrib = contrib[:, :, :, :elems_z]
    column_part = shifted(contrib[:, :, elems_y:], "help", 1)
    forces = jnp.concatenate([contrib[:, :, :1] + column_part, contrib[:, :, 1:elems_y]], axis=2)
    row_part = shifted(forces[:, elems_x:], "dom", 1)
    forces = jnp.concatenate([forces[:, :1] + row_part, forces[:, 1:elems_x]], axis=1)
    return (forces, stress_pts.reshape(elems_x, elems_y, elems_z, 6))


def solution(mesh):
    placed = (
        P(None, "dom", "help", None),
        P("dom", "help", None, None, None),
        P("dom", "help", None, None, None),
        P(),
        P("dom", "help", None),
        P("dom", "help"),
    )
    return jax.shard_map(
        local,
        mesh=mesh,
        in_specs=placed,
        out_specs=(P(None, "dom", "help", None), P("dom", "help", None, None)),
        check_vma=False,
    )
```

profile of v0, /device:TPU:25, one launch (start us, length us, event | category | flops | bytes accessed | tf_op | source)
XLA Modules:
  0.0 543.4 jit_solution(1871092645260940180)
XLA Ops:
  1.3 2.6 collective-permute-start
  6.5 7.8 %all-reduce.27 = s32[16]{0:T(128)S(1)} all-reduce(s32[16]{0:T(128)S(1)} %bitcast_dynamic-update-slice_fusion), channel_id=1, replica_groups=mesh['dom'=2,'help'=16] {'help'}, use_global_device_ids=true, to_apply=%add.27 | all-reduce | flops 16 | bytes 128 | tf_op jit(solution)/shard_map/reshape | solution.py:241
  18.4 4.1 collective-permute-start.1
  22.5 12.2 %copy.37 = f32[2,4,16,7,4096]{4,2,1,0,3:T(8,128)} copy(f32[2,4,16,7,4096]{4,2,3,1,0:T(8,128)} %param.8) | data formatting | bytes 29360128 | tf_op args[1]
  34.8 17.5 %copy.91 = f32[112,8,16,256]{3,2,1,0:T(8,128)} copy(f32[112,8,16,256]{3,1,2,0:T(8,128)} %bitcast.239) | data formatting | bytes 29360128
  52.3 11.9 %gather_fusion.1 = f32[128,7,16,256]{3,2,1,0:T(8,128)} fusion(f32[128,7,16,256]{3,2,0,1:T(8,128)} %bitcast.240, s32[1024]{0:T(1024)S(1)} %pad_clamp_fusion.1), kind=kCustom, calls=%fused_computation.1 | custom fusion | bytes 29360640 | tf_op jit(solution)/shard_map/gather | solution.py:251
  66.0 5.2 all-to-all-start.1
  71.2 13.2 %broadcast_select_fusion = f32[16,8,7,16,256]{4,3,2,1,0:T(8,128)} fusion(f32[16,8,7,16,256]{4,3,2,1,0:T(8,128)} %bitcast.241, pred[16,8]{1,0:T(8,128)(4,1)S(1)} %add_compare_fusion), kind=kLoop, calls=%fused_computation.5 | loop fusion | flops 3670016 | bytes 29360256 | tf_op jit(solution)/shard_map/jit(_where)/select_n | solution.py:251
  84.4 6.5 %all-to-all-start = ((f32[16,8,7,16,256]{4,3,2,1,0:T(8,128)}), f32[16,8,7,16,256]{4,3,2,1,0:T(8,128)}, u32[]{:S(2)}, u32[]{:S(2)}) async-start(f32[16,8,7,16,256]{4,3,2,1,0:T(8,128)} %broadcast_select_fusion), calls=%async_computation | async-start | bytes 29360128 | tf_op jit(solution)/shard_map/all_to_all | solution.py:266
  93.1 4.4 compare_select_fusion.5
  98.2 5.7 %fusion.369 = (f32[256]{0:T(256)S(1)}, f32[256]{0:T(256)S(1)}) fusion(pred[256]{0:T(512)(128)(4,1)S(1)} %compare_reduce_fusion.9, pred[256]{0:T(512)(128)(4,1)S(1)} %compare_reduce_fusion.10, pred[256]{0:T(512)(128)(4,1)S(1)} %compare_reduce_fusion.11, pred[256]{0:T(512)(128)(4,1)S(1)} %compare_reduce_fusion.12, ...), kind=kLoop, calls=%fused_computation.605 | loop fusion | flops 2560 | bytes 5412 | tf_op jit(solution)/shard_map/mul | solution.py:90
  103.9 5.7 %fusion.370 = (f32[256]{0:T(256)S(1)}, f32[256]{0:T(256)S(1)}) fusion(pred[256]{0:T(512)(128)(4,1)S(1)} %compare_reduce_fusion, pred[256]{0:T(512)(128)(4,1)S(1)} %compare_reduce_fusion.1, pred[256]{0:T(512)(128)(4,1)S(1)} %compare_reduce_fusion.2, pred[256]{0:T(512)(128)(4,1)S(1)} %compare_reduce_fusion.3, pred[256]{0:T(512)(128)(4,1)S(1)} %compare_reduce_fusion.4, ...), kind=kLoop, calls=%fused_computation.606 | loop fusion | flops 2560 | bytes 5412 | tf_op jit(solution)/shard_map/mul | solution.py:90
  113.3 284.4 %all-to-all-done = f32[16,8,7,16,256]{4,3,2,1,0:T(8,128)} async-done(((f32[16,8,7,16,256]{4,3,2,1,0:T(8,128)}), f32[16,8,7,16,256]{4,3,2,1,0:T(8,128)}, u32[]{:S(2)}, u32[]{:S(2)}) %all-to-all-start) | async-done | bytes 14680096 | tf_op jit(solution)/shard_map/all_to_all | solution.py:266
  397.7 6.0 %gather_fusion.2 = f32[16,7,16,256]{3,2,1,0:T(8,128)S(1)} fusion(f32[128,7,16,256]{3,2,1,0:T(8,128)} %bitcast.9, s32[1024]{0:T(1024)} %copy-done.14), kind=kCustom, calls=%fused_computation.2 | custom fusion | bytes 3670080 | tf_op jit(solution)/shard_map/gather | solution.py:275
  405.4 2.5 fusion.24
  407.9 2.5 convolution_negate_fusion.2
  415.0 10.4 %subtract_bitcast_fusion.2 = f32[16,6,16,256]{3,2,1,0:T(8,128)S(1)} fusion(f32[16,6,256,16]{2,3,1,0:T(8,128)S(1)} %fusion.139, f32[16,6,16,256]{3,2,1,0:T(8,128)S(1)} %fusion.24), kind=kOutput, calls=%fused_computation.33 | convolution fusion | flops 75894272 | bytes 4718592 | tf_op jit(solution)/shard_map/ak,bcax->bckx/dot_general | solution.py:120
  433.1 2.5 fusion.8
  435.6 2.8 slice_subtract_fusion.1
  439.1 2.5 fusion.65
  441.7 2.5 convolution_negate_fusion.1
  458.6 2.5 fusion.4
  461.1 2.7 slice_subtract_fusion
  464.6 2.5 fusion.62
  467.1 2.5 convolution_negate_fusion
  483.9 2.8 fusion
  486.7 2.6 subtract_subtract_fusion
  496.8 25.1 %all-to-all-start.2 = ((f32[16,8,6]{1,2,0:T(8,128)}), f32[16,8,6]{1,2,0:T(8,128)S(1)}, u32[]{:S(2)}, u32[]{:S(2)}) async-start(f32[16,8,6]{1,2,0:T(8,128)} %copy.51), calls=%async_computation.2 | async-start | bytes 131072 | tf_op jit(solution)/shard_map/all_to_all | solution.py:284
  522.0 3.7 all-to-all-done.2
  526.5 2.2 collective-permute-start.2
  528.8 3.9 collective-permute-done.2
  534.7 7.7 %collective-permute-done.3 = f32[3,1,4,16]{3,2,1,0:T(4,128)S(1)} collective-permute-done((f32[3,1,4,16]{3,2,1,0:T(4,128)S(1)}, f32[3,1,4,16]{3,2,1,0:T(4,128)S(1)}, u32[]{:S(2)}, u32[]{:S(2)}) %collective-permute-start.3) | collective-permute-done | bytes 800 | tf_op jit(solution)/shard_map/ppermute | solution.py:38
  (229 shorter events, 69.9 us)
Async XLA Ops:
  0.6 16.2 %copy-start = (s32[1,1,128]{2,1,0:T(1,128)S(1)}, s32[1,1,128]{2,1,0:T(1,128)}, u32[]{:S(2)}) copy-start(s32[1,1,128]{2,1,0:T(1,128)} %param.11) | copy-start | bytes 1540
  1.3 17.1 %collective-permute-start = (f32[3,1,4,16]{3,2,1,0:T(4,128)S(1)}, f32[3,1,4,16]{3,2,1,0:T(4,128)S(1)}, u32[]{:S(2)}, u32[]{:S(2)}) collective-permute-start(f32[3,1,4,16]{3,2,1,0:T(4,128)S(1)} %slice.345), channel_id=1, source_target_pairs={{16,0},{17,1},{18,2},{19,3},{20,4},{21,5},{22,6},{23,7},{24,8},{25... | collective-permute-start | bytes 2312 | tf_op jit(solution)/shard_map/ppermute | solution.py:38
  16.9 1.4 copy-start.11
  18.1 79.4 %copy-start.6 = (s32[128]{0:T(128)}, s32[128]{0:T(128)S(1)}, u32[]{:S(2)}) copy-start(s32[128]{0:T(128)S(1)} %gather_fusion) | copy-start | bytes 1540
  18.4 45.7 %collective-permute-start.1 = (f32[3,3,1,16]{3,2,1,0:T(1,128)S(1)}, f32[3,3,1,16]{3,2,1,0:T(1,128)S(1)}, u32[]{:S(2)}, u32[]{:S(2)}) collective-permute-start(f32[3,3,1,16]{3,2,1,0:T(1,128)S(1)} %slice.495), channel_id=1, source_target_pairs={{1,0},{2,1},{3,2},{4,3},{5,4},{6,5},{7,6},{8,7},{9,8},{10,9},{11,1... | collective-permute-start | bytes 1736 | tf_op jit(solution)/shard_map/ppermute | solution.py:38
  66.0 18.4 %all-to-all-start.1 = ((f32[16,8,6]{2,1,0:T(8,128)}), f32[16,8,6]{2,1,0:T(8,128)S(1)}, u32[]{:S(2)}, u32[]{:S(2)}) async-start(f32[16,8,6]{2,1,0:T(8,128)} %bitcast_select_fusion), calls=%async_computation.1 | async-start | bytes 131072 | tf_op jit(solution)/shard_map/all_to_all | solution.py:267
  84.3 6.6 %copy-start.8 = (f32[2,4,16,6,6]{2,1,4,3,0:T(4,128)S(1)}, f32[2,4,16,6,6]{2,1,4,3,0:T(4,128)}, u32[]{:S(2)}) copy-start(f32[2,4,16,6,6]{2,1,4,3,0:T(4,128)} %param.9) | copy-start | bytes 55300
  84.3 25.2 %copy-start.13 = (s32[16,256]{1,0:T(8,128)S(1)}, s32[16,256]{1,0:T(8,128)}, u32[]{:S(2)}) copy-start(s32[16,256]{1,0:T(8,128)} %param.10) | copy-start | bytes 49156
  84.4 313.3 %all-to-all-start = ((f32[16,8,7,16,256]{4,3,2,1,0:T(8,128)}), f32[16,8,7,16,256]{4,3,2,1,0:T(8,128)}, u32[]{:S(2)}, u32[]{:S(2)}) async-start(f32[16,8,7,16,256]{4,3,2,1,0:T(8,128)} %broadcast_select_fusion), calls=%async_computation | async-start | bytes 29360128 | tf_op jit(solution)/shard_map/all_to_all | solution.py:266
  91.0 21.2 %copy-start.18 = (pred[128]{0:T(512)(128)(4,1)}, pred[128]{0:T(512)(128)(4,1)S(1)}, u32[]{:S(2)}) copy-start(pred[128]{0:T(512)(128)(4,1)S(1)} %lt.220) | copy-start | bytes 388
  97.6 14.6 %copy-start.14 = (s32[1024]{0:T(1024)}, s32[1024]{0:T(1024)S(1)}, u32[]{:S(2)}) copy-start(s32[1024]{0:T(1024)S(1)} %pad_clamp_fusion) | copy-start | bytes 12292
  403.6 0.7 copy-start.2
  404.7 0.7 copy-start.10
  414.9 10.5 %copy-start.3 = (f32[16,256]{1,0:T(8,128)S(1)}, f32[16,256]{1,0:T(8,128)}, u32[]{:S(2)}) copy-start(f32[16,256]{1,0:T(8,128)} %get-tuple-element.107) | copy-start | bytes 49156
  415.0 10.5 %copy-start.4 = (f32[16,256]{1,0:T(8,128)S(1)}, f32[16,256]{1,0:T(8,128)}, u32[]{:S(2)}) copy-start(f32[16,256]{1,0:T(8,128)} %get-tuple-element.116) | copy-start | bytes 49156
  415.0 10.5 %copy-start.5 = (f32[16,256]{1,0:T(8,128)S(1)}, f32[16,256]{1,0:T(8,128)}, u32[]{:S(2)}) copy-start(f32[16,256]{1,0:T(8,128)} %get-tuple-element.120) | copy-start | bytes 49156
  492.6 3.2 copy-start.17
  492.6 29.3 %copy-start.9 = (f32[128,6,6]{0,2,1:T(8,128)S(1)}, f32[128,6,6]{0,2,1:T(8,128)}, u32[]{:S(2)}) copy-start(f32[128,6,6]{0,2,1:T(8,128)} %reshape.618) | copy-start | bytes 55300
  492.6 29.3 %copy-start.12 = (f32[128,6]{0,1:T(8,128)S(1)}, f32[128,6]{0,1:T(8,128)}, u32[]{:S(2)}) copy-start(f32[128,6]{0,1:T(8,128)} %copy.89) | copy-start | bytes 9220
  492.6 29.3 %copy-start.15 = (f32[6,6]{1,0:T(8,128)S(1)}, f32[6,6]{1,0:T(8,128)}, u32[]{:S(2)}) copy-start(f32[6,6]{1,0:T(8,128)} %constant.155.clone) | copy-start | bytes 436
  493.4 32.5 %copy-start.7 = (s32[128]{0:T(128)S(1)}, s32[128]{0:T(128)}, u32[]{:S(2)}) copy-start(s32[128]{0:T(128)} %copy-done.6) | copy-start | bytes 1540
  493.4 32.5 %copy-start.19 = (pred[128]{0:T(512)(128)(4,1)S(1)}, pred[128]{0:T(512)(128)(4,1)}, u32[]{:S(2)}) copy-start(pred[128]{0:T(512)(128)(4,1)} %copy-done.18) | copy-start | bytes 388
  493.4 32.5 %copy-start.20 = (pred[128]{0:T(512)(128)(4,1)S(1)}, pred[128]{0:T(512)(128)(4,1)}, u32[]{:S(2)}) copy-start(pred[128]{0:T(512)(128)(4,1)} %fusion.91) | copy-start | bytes 388
  493.4 32.8 %copy-start.16 = (pred[3]{0:T(512)(128)(4,1)S(1)}, pred[3]{0:T(512)(128)(4,1)}, u32[]{:S(2)}) copy-start(pred[3]{0:T(512)(128)(4,1)} %constant.154.clone.1) | copy-start | bytes 13
  493.4 49.6 %copy-start.1 = (s32[1,1,128]{2,1,0:T(1,128)S(1)}, s32[1,1,128]{2,1,0:T(1,128)}, u32[]{:S(2)}) copy-start(s32[1,1,128]{2,1,0:T(1,128)} %param.11) | copy-start | bytes 1540
  496.8 29.0 %all-to-all-start.2 = ((f32[16,8,6]{1,2,0:T(8,128)}), f32[16,8,6]{1,2,0:T(8,128)S(1)}, u32[]{:S(2)}, u32[]{:S(2)}) async-start(f32[16,8,6]{1,2,0:T(8,128)} %copy.51), calls=%async_computation.2 | async-start | bytes 131072 | tf_op jit(solution)/shard_map/all_to_all | solution.py:284
  526.5 6.2 %collective-permute-start.2 = (f32[3,3,1,16]{3,2,1,0:T(1,128)S(1)}, f32[3,3,1,16]{3,2,1,0:T(1,128)S(1)}, u32[]{:S(2)}, u32[]{:S(2)}) collective-permute-start(f32[3,3,1,16]{3,2,1,0:T(1,128)S(1)} %pad_add_fusion.8), channel_id=1, source_target_pairs={{0,1},{1,2},{2,3},{3,4},{4,5},{5,6},{6,7},{7,8},{8,9},{9,10},{10,1... | collective-permute-start | bytes 1736 | tf_op jit(solution)/shard_map/ppermute | solution.py:38
  532.8 9.6 %collective-permute-start.3 = (f32[3,1,4,16]{3,2,1,0:T(4,128)S(1)}, f32[3,1,4,16]{3,2,1,0:T(4,128)S(1)}, u32[]{:S(2)}, u32[]{:S(2)}) collective-permute-start(f32[3,1,4,16]{3,2,1,0:T(4,128)S(1)} %fusion.159), channel_id=1, source_target_pairs={{0,16},{1,17},{2,18},{3,19},{4,20},{5,21},{6,22},{7,23},{8,24},{9,... | collective-permute-start | bytes 2312 | tf_op jit(solution)/shard_map/ppermute | solution.py:38
where the time goes:
time: 554 us; the launch traced here: 543 us
  waiting for transfers between devices  300 us (54%)
  matrix products  77.4 us (14%)
  local copies, waits for them, and re-layouts  58.6 us (11%)
  other arithmetic  50.3 us (9%)
  starting transfers between devices  46.9 us (8%)
  blocking collectives  7.75 us (1%)
    all_to_all x1, waiting for transfers between devices, local(): lax.all_to_all(send_states, 'help', split_axis=0, concat_axis=0, tiled=True)  284 us
    unnamed x64, local copies, waits for them, and re-layouts  34.5 us
    all_to_all x1, starting transfers between devices, local(): lax.all_to_all(returning, 'help', split_axis=0, concat_axis=0, tiled=True)  25.1 us
    dot_general x3, matrix products, forward(): jnp.einsum('ak,bcax->bckx', sin_one, re_plane, precision=highest)  13.7 us
    select_n x1, other arithmetic, local(): jnp.where(valid_mask[:, :, None, None, None], states[point_index], 0.0)  13.2 us
    gather x1, local copies, waits for them, and re-layouts, local(): states[point_index]  11.9 us
    ppermute x4, waiting for transfers between devices, shifted(): return lax.ppermute(block, axis, route)  11.5 us
  transfers between devices with their start and end apart: 7, of which 4 were waited for; matrix products, arithmetic and copies ran while one was open for 15% of the time, Pallas kernels for 0%

commit v1 on v0

v1 whole, which is shorter than its diff:
```python
import functools
import math

import jax
import jax.numpy as jnp
import numpy as np
from jax import lax
from jax.experimental import pallas as pl
from jax.experimental.pallas import tpu as pltpu
from jax.sharding import PartitionSpec as P

SWEEPS = 3
ALPHA = 1.1328025
BATCH = 8
root_half = math.sqrt(0.5)
root_two = math.sqrt(2.0)
lam_ref = 1.5
mu_ref = 2.0
coupling = (lam_ref + mu_ref) / (mu_ref * (lam_ref + 2.0 * mu_ref))
PAIRS = [(0, 0), (1, 1), (2, 2), (1, 2), (0, 2), (0, 1)]


def plane_order(edge):
    half = edge // 2
    special = [(0, 0), (0, half), (half, 0), (half, half)]
    pairs = []
    for ky in range(edge):
        for kz in range(edge):
            if (ky, kz) in special:
                continue
            if (ky, kz) < ((-ky) % edge, (-kz) % edge):
                pairs.append((ky, kz))
    return pairs, special


def gamma_table(xi):
    square = np.sum(xi * xi, axis=-1, keepdims=True)
    n = np.where(square > 0, xi / np.sqrt(np.maximum(square, 1.0)), 0.0)
    scale = [1.0, 1.0, 1.0, root_two, root_two, root_two]
    out = np.zeros(xi.shape[:-1] + (6, 6))
    eye = np.eye(3)
    for r, (i, j) in enumerate(PAIRS):
        for s, (k, l) in enumerate(PAIRS):
            four = 0.0
            for kk, ll in ((k, l), (l, k)):
                four = four + 0.5 * (
                    0.5 / mu_ref * (eye[j, kk] * n[..., i] * n[..., ll] + eye[i, kk] * n[..., j] * n[..., ll])
                    - coupling * n[..., i] * n[..., j] * n[..., kk] * n[..., ll]
                )
            out[..., r, s] = scale[r] * scale[s] * four
    return out


@functools.lru_cache(None)
def build_tables(edge):
    plane = edge * edge
    lanes = plane // 2
    pairs, special = plane_order(edge)
    freq = pairs + special[:2] + pairs + special[2:]
    y, z = np.divmod(np.arange(plane), edge)
    forward = np.zeros((plane, plane))
    weight = np.ones(plane)
    for lane, (ky, kz) in enumerate(freq):
        angle = 2 * math.pi / edge * ((ky * y + kz * z) % edge)
        is_pair = lane % lanes < len(pairs)
        forward[:, lane] = -np.sin(angle) if is_pair and lane >= lanes else np.cos(angle)
        weight[lane] = 2.0 if is_pair else 1.0
    forward = ALPHA * forward
    backward = forward.T * weight[:, None]
    index = np.arange(edge)
    angle = 2 * math.pi / edge * (np.outer(index, index) % edge)
    eye = np.eye(BATCH)
    cos_x, sin_x = ALPHA * np.kron(np.cos(angle), eye), ALPHA * np.kron(np.sin(angle), eye)
    mix = np.concatenate([cos_x, sin_x], axis=1)
    unmix = np.concatenate([cos_x, -sin_x], axis=1)
    signed = np.where(index < edge // 2, index, index - edge).astype(np.float64)
    ky = np.array([f[0] for f in freq])
    kz = np.array([f[1] for f in freq])

    def at(a, b, c):
        grid = np.stack(np.broadcast_arrays(signed[a][:, None], signed[b][None], signed[c][None]), axis=-1)
        return gamma_table(grid)

    neg = (-index) % edge
    gamma = 0.5 * (at(index, ky, kz) + at(neg, (-ky) % edge, (-kz) % edge)) / (edge * plane * ALPHA**4)
    upper = [gamma[..., r, s] for r in range(6) for s in range(r, 6)]
    green = np.repeat(np.stack(upper), BATCH, axis=1).astype(np.float32)
    bf = jnp.bfloat16
    return (
        forward.astype(bf),
        backward.astype(bf),
        mix.astype(bf),
        unmix.astype(bf),
        green,
        len(pairs),
    )


def slot_of(r, s):
    r, s = min(r, s), max(r, s)
    return r * 6 - r * (r - 1) // 2 + s - r


def solve_kernel(
    pair_count, chunk,
    order_ref, count_ref, history_ref, strain_ref, elastic_ref, maps_ref,
    fwd_ref, bwd_ref, mix_ref, unmix_ref, green_ref,
    out_ref,
    landing, states, eps, tau, spectrum, macro, sems,
):
    edge_rows, plane = maps_ref.shape[1], maps_ref.shape[2]
    edge = edge_rows // BATCH
    half = plane // 2
    voxels = edge * plane
    deep = history_ref.shape[2]
    count = count_ref[0]
    batches = (count + BATCH - 1) // BATCH
    out_ref[...] = elastic_ref[...]

    def point(batch, j):
        return order_ref[jnp.minimum(batch * BATCH + j, count - 1)]

    def copies(batch, slot):
        return [
            pltpu.make_async_copy(
                history_ref.at[point(batch, j) // deep, :, point(batch, j) % deep, :],
                landing.at[slot, :, j, :],
                sems.at[slot, j],
            )
            for j in range(BATCH)
        ]

    for one in copies(0, 0):
        one.start()
    lane = lax.broadcasted_iota(jnp.int32, (edge_rows, half), 1)
    is_special = lane >= pair_count

    def turned(data, sign):
        re, im = data[:, :half], data[:, half:]
        top = jnp.where(is_special, re if sign > 0 else -re, im)
        low = jnp.where(is_special, im if sign > 0 else -im, -re)
        return jnp.concatenate(
            [data, jnp.concatenate([top, low], axis=1)], axis=0
        ).astype(jnp.bfloat16)

    def law(strain, rows):
        elastic = [strain[c] - states[c, rows, :] for c in range(6)]
        trace = elastic[0] + elastic[1] + elastic[2]
        third = trace * (1.0 / 3.0)
        dev = [elastic[c] - third for c in range(3)] + elastic[3:]
        square = dev[0] * dev[0]
        for c in range(1, 6):
            square = square + dev[c] * dev[c]
        gain = maps_ref[0, rows, :] * lax.rsqrt(1.0 + states[6, rows, :] * square)
        return trace * maps_ref[1, rows, :], [gain * d for d in dev]

    def body(batch, carry):
        slot = batch % 2

        @pl.when(batch + 1 < batches)
        def _():
            for one in copies(batch + 1, (batch + 1) % 2):
                one.start()

        for one in copies(batch, slot):
            one.wait()
        for j in range(BATCH):
            macro[pl.ds(j, 1), :] = strain_ref[pl.ds(point(batch, j), 1), :]

        def unpack(a, c_):
            cols = pl.ds(pl.multiple_of(a * plane, plane), plane)
            rows = pl.ds(pl.multiple_of(a * BATCH, BATCH), BATCH)
            block = landing[slot, :, :, cols]
            for c in range(6):
                states[c, rows, :] = block[c]
            ratio = maps_ref[2, rows, :] / (1.0 + block[6])
            states[6, rows, :] = ratio * ratio
            return c_

        lax.fori_loop(0, edge, unpack, 0, unroll=2)
        columns = [jnp.broadcast_to(macro[:, c : c + 1], (BATCH, plane)) for c in range(6)]
        wide = [jnp.concatenate([m] * (chunk // BATCH), axis=0) for m in columns]
        for sweep in range(SWEEPS):
            def polarize(i, c_):
                rows = pl.ds(pl.multiple_of(i * chunk, chunk), chunk)
                strain = wide if sweep == 0 else [eps[c, rows, :] for c in range(6)]
                volume, shear = law(strain, rows)
                if sweep > 0:
                    volume = volume - lam_ref * (strain[0] + strain[1] + strain[2])
                for c in range(6):
                    value = shear[c] + volume if c < 3 else shear[c]
                    if sweep > 0:
                        value = value - (2.0 * mu_ref) * strain[c]
                    tau[c, rows, :] = value.astype(jnp.bfloat16)
                return c_

            lax.fori_loop(0, edge_rows // chunk, polarize, 0, unroll=2)
            for c in range(6):
                flat = jnp.dot(tau[c], fwd_ref[...], preferred_element_type=jnp.float32)
                spectrum[c] = jnp.dot(mix_ref[...], turned(flat, 1), preferred_element_type=jnp.float32)

            def green(i, c_):
                rows = pl.ds(pl.multiple_of(i * BATCH, BATCH), BATCH)
                got = [spectrum[c, rows, :] for c in range(6)]
                done = []
                for r in range(6):
                    total = green_ref[slot_of(r, 0), rows, :] * got[0]
                    for s in range(1, 6):
                        total = total + green_ref[slot_of(r, s), rows, :] * got[s]
                    done.append(total)
                for r in range(6):
                    spectrum[r, rows, :] = done[r]
                return c_

            lax.fori_loop(0, edge, green, 0, unroll=2)
            for c in range(6):
                back = jnp.dot(unmix_ref[...], turned(spectrum[c], -1), preferred_element_type=jnp.float32)
                field = jnp.dot(back.astype(jnp.bfloat16), bwd_ref[...], preferred_element_type=jnp.float32)
                eps[c] = jnp.concatenate([columns[c]] * edge, axis=0) - field

        def average(i, sums):
            rows = pl.ds(pl.multiple_of(i * BATCH, BATCH), BATCH)
            volume, shear = law([eps[c, rows, :] for c in range(6)], rows)
            return tuple(
                sums[c] + (shear[c] + volume if c < 3 else shear[c]) for c in range(6)
            )

        zero = jnp.zeros((BATCH, plane), jnp.float32)
        sums = lax.fori_loop(0, edge, average, (zero,) * 6, unroll=2)
        means = jnp.concatenate(
            [jnp.sum(s, axis=1, keepdims=True) * (1.0 / voxels) for s in sums], axis=1
        )
        for j in range(BATCH):
            out_ref[pl.ds(point(batch, j), 1), :] = means[j : j + 1, :]
        return carry

    lax.fori_loop(0, batches, body, 0)


def solve_points(yield_list, live_count, states, strain_pts, elastic, phases):
    columns, deep, comps, voxels = states.shape
    points = columns * deep
    states = jnp.swapaxes(states, 1, 2)
    edge, plane = phases.shape
    rows = edge * BATCH
    forward, backward, mix, unmix, green, pair_count = build_tables(edge)
    is_hard = (phases == 1).astype(jnp.float32)
    lame, shear, strength = 1.0 + is_hard, 1.0 + 2.0 * is_hard, 0.4 + 0.4 * is_hard
    maps = jnp.repeat(
        jnp.stack([2.0 * shear, lame + 2.0 * shear / 3.0, 2.0 * shear / strength]), BATCH, axis=1
    )
    smem = pl.BlockSpec(memory_space=pltpu.SMEM)
    vmem = pl.BlockSpec(memory_space=pltpu.VMEM)
    return pl.pallas_call(
        functools.partial(solve_kernel, pair_count, 16),
        out_shape=jax.ShapeDtypeStruct((points, 6), jnp.float32),
        in_specs=[smem, smem, pl.BlockSpec(memory_space=pl.ANY)] + [vmem] * 8,
        out_specs=vmem,
        scratch_shapes=[
            pltpu.VMEM((2, comps, BATCH, voxels), jnp.float32),
            pltpu.VMEM((7, rows, plane), jnp.float32),
            pltpu.VMEM((6, rows, plane), jnp.float32),
            pltpu.VMEM((6, rows, plane), jnp.bfloat16),
            pltpu.VMEM((6, rows, plane), jnp.float32),
            pltpu.VMEM((BATCH, 6), jnp.float32),
            pltpu.SemaphoreType.DMA((2, BATCH)),
        ],
        compiler_params=pltpu.CompilerParams(vmem_limit_bytes=48 * 1024 * 1024),
        name="cell_solve",
    )(yield_list, live_count, states, strain_pts, elastic, maps,
      jnp.asarray(forward), jnp.asarray(backward), jnp.asarray(mix), jnp.asarray(unmix), jnp.asarray(green))


highest = lax.Precision.HIGHEST
iso_stiffness = np.array(
    [
        [
            (
                (lam_ref + 2.0 * mu_ref if row_id < 3 else 2.0 * mu_ref)
                if row_id == col_id
                else lam_ref if row_id < 3 and col_id < 3 else 0.0
            )
            for col_id in range(6)
        ]
        for row_id in range(6)
    ],
    dtype=np.float32,
)


def shifted(block, axis, distance):
    devices = range(lax.axis_size(axis))
    route = [(i - distance, i) for i in devices if i - distance in devices]
    return lax.ppermute(block, axis, route)


def strain_map(extended):
    diff_x = extended[:, 1:] - extended[:, :-1]
    grad_x = 0.25 * (
        diff_x[:, :, :-1, :-1]
        + diff_x[:, :, 1:, :-1]
        + diff_x[:, :, :-1, 1:]
        + diff_x[:, :, 1:, 1:]
    )
    diff_y = extended[:, :, 1:] - extended[:, :, :-1]
    grad_y = 0.25 * (
        diff_y[:, :-1, :, :-1]
        + diff_y[:, 1:, :, :-1]
        + diff_y[:, :-1, :, 1:]
        + diff_y[:, 1:, :, 1:]
    )
    diff_z = extended[:, :, :, 1:] - extended[:, :, :, :-1]
    grad_z = 0.25 * (
        diff_z[:, :-1, :-1] + diff_z[:, 1:, :-1] + diff_z[:, :-1, 1:] + diff_z[:, 1:, 1:]
    )
    return jnp.stack(
        [
            grad_x[0],
            grad_y[1],
            grad_z[2],
            root_half * (grad_z[1] + grad_y[2]),
            root_half * (grad_z[0] + grad_x[2]),
            root_half * (grad_y[0] + grad_x[1]),
        ]
    )


def local(displacement, history, stored_stiffness, phases, yield_order, yield_count):
    elems_x = displacement.shape[1]
    elems_y = displacement.shape[2]
    elems_z = displacement.shape[3]
    points = elems_x * elems_y * elems_z
    yield_list = yield_order.reshape(points)
    live_count = yield_count.reshape(1)
    upper_row = shifted(displacement[:, :1], "dom", -1)
    extended = jnp.concatenate([displacement, upper_row], axis=1)
    upper_column = shifted(extended[:, :, :1], "help", -1)
    extended = jnp.concatenate([extended, upper_column], axis=2)
    extended = jnp.pad(extended, ((0, 0), (0, 0), (0, 0), (0, 1)))
    strain, pullback = jax.vjp(strain_map, extended)
    strain_pts = jnp.transpose(strain, (1, 2, 3, 0)).reshape(points, 6)
    stiffness = stored_stiffness.reshape(points, 6, 6) + jnp.asarray(
        iso_stiffness, dtype=stored_stiffness.dtype
    )
    elastic = jnp.einsum("pij,pj->pi", stiffness, strain_pts, precision=highest)
    states = history.reshape(elems_x * elems_y, elems_z, history.shape[3], history.shape[4])
    stress_pts = solve_points(yield_list, live_count, states, strain_pts, elastic, phases)
    stress_field = jnp.transpose(stress_pts.reshape(elems_x, elems_y, elems_z, 6), (3, 0, 1, 2))
    (contrib,) = pullback(stress_field)
    contrib = contrib[:, :, :, :elems_z]
    column_part = shifted(contrib[:, :, elems_y:], "help", 1)
    forces = jnp.concatenate([contrib[:, :, :1] + column_part, contrib[:, :, 1:elems_y]], axis=2)
    row_part = shifted(forces[:, elems_x:], "dom", 1)
    forces = jnp.concatenate([forces[:, :1] + row_part, forces[:, 1:elems_x]], axis=1)
    return (forces, stress_pts.reshape(elems_x, elems_y, elems_z, 6))


def solution(mesh):
    placed = (
        P(None, "dom", "help", None),
        P("dom", "help", None, None, None),
        P("dom", "help", None, None, None),
        P(),
        P("dom", "help", None),
        P("dom", "help"),
    )
    return jax.shard_map(
        local,
        mesh=mesh,
        in_specs=placed,
        out_specs=(P(None, "dom", "help", None), P("dom", "help", None, None)),
        check_vma=False,
    )
```

time: 554 us -> 121 us (0.22); the launches traced: 543 us -> 122 us
  waiting for transfers between devices: 300 us -> 88.2 us
  matrix products: 77.4 us -> 0.97 us
  local copies, waits for them, and re-layouts: 58.6 us -> 9.69 us
  other arithmetic: 50.3 us -> 2.99 us
  starting transfers between devices: 46.9 us -> 10.5 us
  blocking collectives: 7.75 us -> 0 us
  Pallas kernels: 0 us -> 7.7 us
    all_to_all x3 -> x0, waiting for transfers between devices: 288 us -> none  [the longest x1 284 us: local(): lax.all_to_all(send_states, 'help', split_axis=0, concat_axis=0, tiled=True)]
    ppermute x4, waiting for transfers between devices: 11.5 us -> 88.2 us  [shifted(): return lax.ppermute(block, axis, route)]
    dot_general x38 -> x1, matrix products: 77.4 us -> 0.97 us  [local(): elastic = jnp.einsum('pij,pj->pi', stiffness, strain_pts, precision=highest)]
    all_to_all x3 -> x0, starting transfers between devices: 36.8 us -> none  [the longest x1 25.1 us: local(): lax.all_to_all(returning, 'help', split_axis=0, concat_axis=0, tiled=True)]
    unnamed x64 -> x20, local copies, waits for them, and re-layouts: 34.5 us -> 8.32 us
    gather x7 -> x0, local copies, waits for them, and re-layouts: 21 us -> none  [the longest x1 11.9 us: local(): states[point_index]]
    select_n x7 -> x0, other arithmetic: 14.7 us -> none  [the longest x1 13.2 us: local(): jnp.where(valid_mask[:, :, None, None, None], states[point_index], 0.0)]
    mul x7 -> x0, other arithmetic: 13.3 us -> none  [the longest x1 5.67 us: direction_table(): third_dir * third_dir]
  transfers between devices with their start and end apart: 7 -> 4, of which waited for: 4 -> 2; matrix products, arithmetic and copies ran while one was open for 15% -> 4% of each run, Pallas kernels for 0% -> 0%
where the time goes in v1:
time: 121 us; the launch traced here: 122 us
  waiting for transfers between devices  88.2 us (73%)
  starting transfers between devices  10.5 us (9%)
  local copies, waits for them, and re-layouts  9.69 us (8%)
  Pallas kernels  7.7 us (6%)
  other arithmetic  2.99 us (2%)
  between operations  1.49 us (1%)
    ppermute x4, waiting for transfers between devices, shifted(): return lax.ppermute(block, axis, route)  88.2 us
    ppermute x4, starting transfers between devices, shifted(): return lax.ppermute(block, axis, route)  10.5 us
    unnamed x20, local copies, waits for them, and re-layouts  8.32 us
    pallas_call x1, Pallas kernels, solve_points(): pl.pallas_call(functools.partial(solve_kernel, pair_count, 16), out_shape...  7.7 us
  transfers between devices with their start and end apart: 4, of which 2 were waited for; matrix products, arithmetic and copies ran while one was open for 4% of the time, Pallas kernels for 0%

profile of v1, /device:TPU:25, one launch (start us, length us, event | category | flops | bytes accessed | tf_op | source)
XLA Modules:
  0.0 121.6 jit_solution(6652811967562781019)
XLA Ops:
  0.6 0.7 slice.110
  1.3 2.6 %collective-permute-start = (f32[3,1,4,16]{3,2,1,0:T(4,128)S(1)}, f32[3,1,4,16]{3,2,1,0:T(4,128)S(1)}, u32[]{:S(2)}, u32[]{:S(2)}) collective-permute-start(f32[3,1,4,16]{3,2,1,0:T(4,128)S(1)} %slice.110), channel_id=1, source_target_pairs={{16,0},{17,1},{18,2},{19,3},{20,4},{21,5},{22,6},{23,7},{24,8},{25... | collective-permute-start | bytes 2312 | tf_op jit(solution)/shard_map/ppermute | solution.py:294
  3.9 0.7 fusion.3
  4.7 0.7 constant_dynamic-update-slice_fusion.1
  5.4 0.9 copy.18
  6.4 0.1 reshape.31
  6.5 4.0 %collective-permute-start.1 = (f32[3,3,1,16]{3,2,1,0:T(1,128)S(1)}, f32[3,3,1,16]{3,2,1,0:T(1,128)S(1)}, u32[]{:S(2)}, u32[]{:S(2)}) collective-permute-start(f32[3,3,1,16]{3,2,1,0:T(1,128)S(1)} %slice.145), channel_id=1, source_target_pairs={{1,0},{2,1},{3,2},{4,3},{5,4},{6,5},{7,6},{8,7},{9,8},{10,9},{11,1... | collective-permute-start | bytes 1736 | tf_op jit(solution)/shard_map/ppermute | solution.py:294
  10.5 0.8 broadcast_add_fusion
  11.3 0.3 copy.21
  12.3 0.1 fusion.9
  12.4 0.1 fusion.7
  12.6 0.1 copy.17
  12.7 1.0 fusion.20
  13.7 1.8 %copy-done = f32[21,128,256]{2,1,0:T(8,128)S(1)} copy-done((f32[21,128,256]{2,1,0:T(8,128)S(1)}, f32[21,128,256]{2,1,0:T(8,128)}, u32[]{:S(2)}) %copy-start) | copy-done | bytes 2752536
  15.5 0.9 copy-done.1
  16.4 0.9 copy-done.2
  17.3 0.8 copy-done.3
  18.1 0.8 copy-done.4
  18.9 0.7 copy-done.5
  19.6 7.7 %cell_solve.1 = f32[128,6]{1,0:T(8,128)S(1)} custom-call(s32[128]{0:T(128)S(1)} %bitcast.33, s32[1]{0:T(128)} %bitcast.27.count_ref, f32[8,7,16,4096]{3,2,1,0:T(8,128)} %bitcast.34, f32[128,6]{1,0:T(8,128)S(1)} %bitcast.29, f32[128,6]{1,0:T(8,128)S(1)} %bitcast.32, f32[3,128,256]{2,1,0:T(8,128)S(1)} %broadcast_bitcast_fusion.maps_ref, ...), custom_call_target="tpu_custom_call" | custom-call | tf_op jit(solution)/shard_map/cell_solve/pallas_call | solution.py:254
  27.3 0.1 copy.19
  27.4 0.1 add_multiply_fusion.1
  27.5 0.1 fusion.17
  27.7 0.1 pad_add_fusion.8
  27.8 2.7 %collective-permute-start.2 = (f32[3,3,1,16]{3,2,1,0:T(1,128)S(1)}, f32[3,3,1,16]{3,2,1,0:T(1,128)S(1)}, u32[]{:S(2)}, u32[]{:S(2)}) collective-permute-start(f32[3,3,1,16]{3,2,1,0:T(1,128)S(1)} %pad_add_fusion.8), channel_id=1, source_target_pairs={{0,1},{1,2},{2,3},{3,4},{4,5},{5,6},{6,7},{7,8},{8,9},{9,10},{10,1... | collective-permute-start | bytes 1736 | tf_op jit(solution)/shard_map/ppermute | solution.py:294
  30.5 0.1 pad_add_fusion.2
  30.6 87.2 %collective-permute-done.2 = f32[3,3,1,16]{3,2,1,0:T(1,128)S(1)} collective-permute-done((f32[3,3,1,16]{3,2,1,0:T(1,128)S(1)}, f32[3,3,1,16]{3,2,1,0:T(1,128)S(1)}, u32[]{:S(2)}, u32[]{:S(2)}) %collective-permute-start.2) | collective-permute-done | bytes 608 | tf_op jit(solution)/shard_map/ppermute | solution.py:294
  117.8 0.1 add_add_fusion
  117.9 1.3 %collective-permute-start.3 = (f32[3,1,4,16]{3,2,1,0:T(4,128)S(1)}, f32[3,1,4,16]{3,2,1,0:T(4,128)S(1)}, u32[]{:S(2)}, u32[]{:S(2)}) collective-permute-start(f32[3,1,4,16]{3,2,1,0:T(4,128)S(1)} %fusion.10), channel_id=1, source_target_pairs={{0,16},{1,17},{2,18},{3,19},{4,20},{5,21},{6,22},{7,23},{8,24},{9,... | collective-permute-start | bytes 2312 | tf_op jit(solution)/shard_map/ppermute | solution.py:294
  119.2 0.7 copy.20
  119.9 1.0 collective-permute-done.3
  120.9 0.6 fusion.4
  (30 shorter events, 0.4 us)
Async XLA Ops:
  0.6 26.8 %copy-start.6 = (pred[3]{0:T(512)(128)(4,1)S(1)}, pred[3]{0:T(512)(128)(4,1)}, u32[]{:S(2)}) copy-start(pred[3]{0:T(512)(128)(4,1)} %constant.35.clone.1) | copy-start | bytes 13
  1.3 5.2 %collective-permute-start = (f32[3,1,4,16]{3,2,1,0:T(4,128)S(1)}, f32[3,1,4,16]{3,2,1,0:T(4,128)S(1)}, u32[]{:S(2)}, u32[]{:S(2)}) collective-permute-start(f32[3,1,4,16]{3,2,1,0:T(4,128)S(1)} %slice.110), channel_id=1, source_target_pairs={{16,0},{17,1},{18,2},{19,3},{20,4},{21,5},{22,6},{23,7},{24,8},{25... | collective-permute-start | bytes 2312 | tf_op jit(solution)/shard_map/ppermute | solution.py:294
  6.5 5.7 %collective-permute-start.1 = (f32[3,3,1,16]{3,2,1,0:T(1,128)S(1)}, f32[3,3,1,16]{3,2,1,0:T(1,128)S(1)}, u32[]{:S(2)}, u32[]{:S(2)}) collective-permute-start(f32[3,3,1,16]{3,2,1,0:T(1,128)S(1)} %slice.145), channel_id=1, source_target_pairs={{1,0},{2,1},{3,2},{4,3},{5,4},{6,5},{7,6},{8,7},{9,8},{10,9},{11,1... | collective-permute-start | bytes 1736 | tf_op jit(solution)/shard_map/ppermute | solution.py:294
  13.7 1.8 %copy-start = (f32[21,128,256]{2,1,0:T(8,128)S(1)}, f32[21,128,256]{2,1,0:T(8,128)}, u32[]{:S(2)}) copy-start(f32[21,128,256]{2,1,0:T(8,128)} %constant.41.clone.green_ref) | copy-start | bytes 8257540
  15.5 0.9 copy-start.1
  16.4 0.9 copy-start.2
  17.3 0.8 copy-start.3
  18.1 0.8 copy-start.4
  18.9 0.7 copy-start.5
  27.8 90.0 %collective-permute-start.2 = (f32[3,3,1,16]{3,2,1,0:T(1,128)S(1)}, f32[3,3,1,16]{3,2,1,0:T(1,128)S(1)}, u32[]{:S(2)}, u32[]{:S(2)}) collective-permute-start(f32[3,3,1,16]{3,2,1,0:T(1,128)S(1)} %pad_add_fusion.8), channel_id=1, source_target_pairs={{0,1},{1,2},{2,3},{3,4},{4,5},{5,6},{6,7},{7,8},{8,9},{9,10},{10,1... | collective-permute-start | bytes 1736 | tf_op jit(solution)/shard_map/ppermute | solution.py:294
  117.9 3.1 %collective-permute-start.3 = (f32[3,1,4,16]{3,2,1,0:T(4,128)S(1)}, f32[3,1,4,16]{3,2,1,0:T(4,128)S(1)}, u32[]{:S(2)}, u32[]{:S(2)}) collective-permute-start(f32[3,1,4,16]{3,2,1,0:T(4,128)S(1)} %fusion.10), channel_id=1, source_target_pairs={{0,16},{1,17},{2,18},{3,19},{4,20},{5,21},{6,22},{7,23},{8,24},{9,... | collective-permute-start | bytes 2312 | tf_op jit(solution)/shard_map/ppermute | solution.py:294

commit v2 on v1

--- a/solution.py
+++ b/solution.py
@@ -10,8 +10,9 @@
 from jax.sharding import PartitionSpec as P
 
 SWEEPS = 3
-ALPHA = 1.1328025
 BATCH = 8
+UNROLL = 4
+GUNROLL = 8
 root_half = math.sqrt(0.5)
 root_two = math.sqrt(2.0)
 lam_ref = 1.5
@@ -65,12 +66,11 @@
         is_pair = lane % lanes < len(pairs)
         forward[:, lane] = -np.sin(angle) if is_pair and lane >= lanes else np.cos(angle)
         weight[lane] = 2.0 if is_pair else 1.0
-    forward = ALPHA * forward
     backward = forward.T * weight[:, None]
     index = np.arange(edge)
     angle = 2 * math.pi / edge * (np.outer(index, index) % edge)
     eye = np.eye(BATCH)
-    cos_x, sin_x = ALPHA * np.kron(np.cos(angle), eye), ALPHA * np.kron(np.sin(angle), eye)
+    cos_x, sin_x = np.kron(np.cos(angle), eye), np.kron(np.sin(angle), eye)
     mix = np.concatenate([cos_x, sin_x], axis=1)
     unmix = np.concatenate([cos_x, -sin_x], axis=1)
     signed = np.where(index < edge // 2, index, index - edge).astype(np.float64)
@@ -82,15 +82,22 @@
         return gamma_table(grid)
 
     neg = (-index) % edge
-    gamma = 0.5 * (at(index, ky, kz) + at(neg, (-ky) % edge, (-kz) % edge)) / (edge * plane * ALPHA**4)
+    gamma = 0.5 * (at(index, ky, kz) + at(neg, (-ky) % edge, (-kz) % edge)) / (edge * plane)
     upper = [gamma[..., r, s] for r in range(6) for s in range(r, 6)]
     green = np.repeat(np.stack(upper), BATCH, axis=1).astype(np.float32)
-    bf = jnp.bfloat16
+    def parts(table):
+        high = table.astype(jnp.bfloat16)
+        return high, (table - high.astype(np.float64)).astype(jnp.bfloat16)
+
+    def three(table):
+        high, low = parts(table)
+        return np.concatenate([high, high, low], axis=0)
+
     return (
-        forward.astype(bf),
-        backward.astype(bf),
-        mix.astype(bf),
-        unmix.astype(bf),
+        three(forward),
+        three(backward),
+        np.concatenate(parts(mix), axis=0),
+        np.concatenate(parts(unmix), axis=0),
         green,
         len(pairs),
     )
@@ -106,7 +113,7 @@
     order_ref, count_ref, history_ref, strain_ref, elastic_ref, maps_ref,
     fwd_ref, bwd_ref, mix_ref, unmix_ref, green_ref,
     out_ref,
-    landing, states, eps, tau, spectrum, macro, sems,
+    landing, states, pair, wave, spectrum, macro, sems,
 ):
     edge_rows, plane = maps_ref.shape[1], maps_ref.shape[2]
     edge = edge_rows // BATCH
@@ -132,16 +139,27 @@
 
     for one in copies(0, 0):
         one.start()
-    lane = lax.broadcasted_iota(jnp.int32, (edge_rows, half), 1)
-    is_special = lane >= pair_count
-
     def turned(data, sign):
         re, im = data[:, :half], data[:, half:]
+        lane = lax.broadcasted_iota(jnp.int32, re.shape, 1)
+        is_special = lane >= pair_count
         top = jnp.where(is_special, re if sign > 0 else -re, im)
         low = jnp.where(is_special, im if sign > 0 else -im, -re)
-        return jnp.concatenate(
-            [data, jnp.concatenate([top, low], axis=1)], axis=0
-        ).astype(jnp.bfloat16)
+        return jnp.concatenate([top, low], axis=1)
+
+    def split(data):
+        high = data.astype(jnp.bfloat16)
+        return high, (data - high.astype(jnp.float32)).astype(jnp.bfloat16)
+
+    def plane_dot(high, low, table_ref):
+        return jnp.dot(
+            jnp.concatenate([high, low, high], axis=1), table_ref[...], preferred_element_type=jnp.float32
+        )
+
+    def axis_dot(table_ref, c):
+        both = jnp.dot(table_ref[...], pair[0, c], preferred_element_type=jnp.float32)
+        rest = jnp.dot(table_ref[:edge_rows], pair[1, c], preferred_element_type=jnp.float32)
+        return both[:edge_rows] + (both[edge_rows:] + rest)
 
     def law(strain, rows):
         elastic = [strain[c] - states[c, rows, :] for c in range(6)]
@@ -180,53 +198,66 @@
         lax.fori_loop(0, edge, unpack, 0, unroll=2)
         columns = [jnp.broadcast_to(macro[:, c : c + 1], (BATCH, plane)) for c in range(6)]
         wide = [jnp.concatenate([m] * (chunk // BATCH), axis=0) for m in columns]
+
+        def strain_at(rows):
+            high, low = (
+                jnp.concatenate([wave[k, c, rows, :] for c in range(6)], axis=0) for k in range(2)
+            )
+            field = plane_dot(high, low, bwd_ref)
+            return [wide[c] - field[c * chunk : (c + 1) * chunk] for c in range(6)]
+
         for sweep in range(SWEEPS):
             def polarize(i, c_):
                 rows = pl.ds(pl.multiple_of(i * chunk, chunk), chunk)
-                strain = wide if sweep == 0 else [eps[c, rows, :] for c in range(6)]
+                low = pl.ds(pl.multiple_of(edge_rows + i * chunk, chunk), chunk)
+                strain = wide if sweep == 0 else strain_at(rows)
                 volume, shear = law(strain, rows)
                 if sweep > 0:
                     volume = volume - lam_ref * (strain[0] + strain[1] + strain[2])
+                parts = []
                 for c in range(6):
                     value = shear[c] + volume if c < 3 else shear[c]
                     if sweep > 0:
                         value = value - (2.0 * mu_ref) * strain[c]
-                    tau[c, rows, :] = value.astype(jnp.bfloat16)
+                    parts.append(value)
+                flat = plane_dot(*split(jnp.concatenate(parts, axis=0)), fwd_ref)
+                for c in range(6):
+                    for k, piece in enumerate(split(flat[c * chunk : (c + 1) * chunk])):
+                        pair[k, c, rows, :] = piece
+                        pair[k, c, low, :] = turned(piece, 1)
                 return c_
 
-            lax.fori_loop(0, edge_rows // chunk, polarize, 0, unroll=2)
+            lax.fori_loop(0, edge_rows // chunk, polarize, 0, unroll=UNROLL)
             for c in range(6):
-                flat = jnp.dot(tau[c], fwd_ref[...], preferred_element_type=jnp.float32)
-                spectrum[c] = jnp.dot(mix_ref[...], turned(flat, 1), preferred_element_type=jnp.float32)
+                spectrum[c] = axis_dot(mix_ref, c)
 
             def green(i, c_):
-                rows = pl.ds(pl.multiple_of(i * BATCH, BATCH), BATCH)
+                rows = pl.ds(pl.multiple_of(i * 16, 16), 16)
+                low = pl.ds(pl.multiple_of(edge_rows + i * 16, 16), 16)
                 got = [spectrum[c, rows, :] for c in range(6)]
-                done = []
                 for r in range(6):
                     total = green_ref[slot_of(r, 0), rows, :] * got[0]
                     for s in range(1, 6):
                         total = total + green_ref[slot_of(r, s), rows, :] * got[s]
-                    done.append(total)
-                for r in range(6):
-                    spectrum[r, rows, :] = done[r]
+                    for k, piece in enumerate(split(total)):
+                        pair[k, r, rows, :] = piece
+                        pair[k, r, low, :] = turned(piece, -1)
                 return c_
 
-            lax.fori_loop(0, edge, green, 0, unroll=2)
+            lax.fori_loop(0, edge_rows // 16, green, 0, unroll=GUNROLL)
             for c in range(6):
-                back = jnp.dot(unmix_ref[...], turned(spectrum[c], -1), preferred_element_type=jnp.float32)
-                field = jnp.dot(back.astype(jnp.bfloat16), bwd_ref[...], preferred_element_type=jnp.float32)
-                eps[c] = jnp.concatenate([columns[c]] * edge, axis=0) - field
+                wave[0, c], wave[1, c] = split(axis_dot(unmix_ref, c))
 
         def average(i, sums):
-            rows = pl.ds(pl.multiple_of(i * BATCH, BATCH), BATCH)
-            volume, shear = law([eps[c, rows, :] for c in range(6)], rows)
+            rows = pl.ds(pl.multiple_of(i * chunk, chunk), chunk)
+            volume, shear = law(strain_at(rows), rows)
             return tuple(
                 sums[c] + (shear[c] + volume if c < 3 else shear[c]) for c in range(6)
             )
 
-        zero = jnp.zeros((BATCH, plane), jnp.float32)
-        sums = lax.fori_loop(0, edge, average, (zero,) * 6, unroll=2)
+        zero = jnp.zeros((chunk, plane), jnp.float32)
+        sums = lax.fori_loop(0, edge_rows // chunk, average, (zero,) * 6, unroll=UNROLL)
+        sums = [sum(s[k : k + BATCH] for k in range(0, chunk, BATCH)) for s in sums]
         means = jnp.concatenate(
             [jnp.sum(s, axis=1, keepdims=True) * (1.0 / voxels) for s in sums], axis=1
         )
@@ -252,15 +283,15 @@
     smem = pl.BlockSpec(memory_space=pltpu.SMEM)
     vmem = pl.BlockSpec(memory_space=pltpu.VMEM)
     return pl.pallas_call(
-        functools.partial(solve_kernel, pair_count, 16),
+        functools.partial(solve_kernel, pair_count, 32),
         out_shape=jax.ShapeDtypeStruct((points, 6), jnp.float32),
         in_specs=[smem, smem, pl.BlockSpec(memory_space=pl.ANY)] + [vmem] * 8,
         out_specs=vmem,
         scratch_shapes=[
             pltpu.VMEM((2, comps, BATCH, voxels), jnp.float32),
             pltpu.VMEM((7, rows, plane), jnp.float32),
-            pltpu.VMEM((6, rows, plane), jnp.float32),
-            pltpu.VMEM((6, rows, plane), jnp.bfloat16),
+            pltpu.VMEM((2, 6, 2 * rows, plane), jnp.bfloat16),
+            pltpu.VMEM((2, 6, rows, plane), jnp.bfloat16),
             pltpu.VMEM((6, rows, plane), jnp.float32),
             pltpu.VMEM((BATCH, 6), jnp.float32),
             pltpu.SemaphoreType.DMA((2, BATCH)),

time: 121 us -> 146 us (1.21)
  waiting for transfers between devices: 88.2 us -> 110 us
  Pallas kernels: 7.7 us -> 9.3 us
    ppermute x4, waiting for transfers between devices: 88.2 us -> 110 us  [shifted(): return lax.ppermute(block, axis, route)]
    pallas_call x1, Pallas kernels: 7.7 us -> 9.3 us  [solve_points(): pl.pallas_call(functools.partial(solve_kernel, pair_count, 32), out_shape...]
  transfers between devices with their start and end apart: 4 -> 4, of which waited for: 2 -> 2; matrix products, arithmetic and copies ran while one was open for 4% -> 3% of each run, Pallas kernels for 0% -> 0%
where the time goes in v2:
time: 146 us; the launch traced here: 145 us
  waiting for transfers between devices  110 us (75%)
  starting transfers between devices  10.3 us (7%)
  local copies, waits for them, and re-layouts  10 us (7%)
  Pallas kernels  9.3 us (6%)
  other arithmetic  2.99 us (2%)
  between operations  1.49 us (1%)
    ppermute x4, waiting for transfers between devices, shifted(): return lax.ppermute(block, axis, route)  110 us
    ppermute x4, starting transfers between devices, shifted(): return lax.ppermute(block, axis, route)  10.3 us
    pallas_call x1, Pallas kernels, solve_points(): pl.pallas_call(functools.partial(solve_kernel, pair_count, 32), out_shape...  9.3 us
    unnamed x20, local copies, waits for them, and re-layouts  8.63 us
  transfers between devices with their start and end apart: 4, of which 2 were waited for; matrix products, arithmetic and copies ran while one was open for 3% of the time, Pallas kernels for 0%

profile of v2, /device:TPU:25, one launch (start us, length us, event | category | flops | bytes accessed | tf_op | source)
XLA Modules:
  0.0 145.3 jit_solution(17260306030939980593)
XLA Ops:
  0.6 0.7 slice.110
  1.3 2.6 %collective-permute-start = (f32[3,1,4,16]{3,2,1,0:T(4,128)S(1)}, f32[3,1,4,16]{3,2,1,0:T(4,128)S(1)}, u32[]{:S(2)}, u32[]{:S(2)}) collective-permute-start(f32[3,1,4,16]{3,2,1,0:T(4,128)S(1)} %slice.110), channel_id=1, source_target_pairs={{16,0},{17,1},{18,2},{19,3},{20,4},{21,5},{22,6},{23,7},{24,8},{25... | collective-permute-start | bytes 2312 | tf_op jit(solution)/shard_map/ppermute | solution.py:325
  3.9 0.7 fusion.3
  4.7 0.7 constant_dynamic-update-slice_fusion.1
  5.4 0.9 copy.18
  6.4 0.1 reshape.31
  6.5 4.0 %collective-permute-start.1 = (f32[3,3,1,16]{3,2,1,0:T(1,128)S(1)}, f32[3,3,1,16]{3,2,1,0:T(1,128)S(1)}, u32[]{:S(2)}, u32[]{:S(2)}) collective-permute-start(f32[3,3,1,16]{3,2,1,0:T(1,128)S(1)} %slice.145), channel_id=1, source_target_pairs={{1,0},{2,1},{3,2},{4,3},{5,4},{6,5},{7,6},{8,7},{9,8},{10,9},{11,1... | collective-permute-start | bytes 1736 | tf_op jit(solution)/shard_map/ppermute | solution.py:325
  10.5 0.8 broadcast_add_fusion
  11.3 0.3 copy.21
  12.3 0.1 fusion.9
  12.4 0.1 fusion.7
  12.6 0.1 copy.17
  12.7 1.0 fusion.20
  13.7 1.8 %copy-done = f32[21,128,256]{2,1,0:T(8,128)S(1)} copy-done((f32[21,128,256]{2,1,0:T(8,128)S(1)}, f32[21,128,256]{2,1,0:T(8,128)}, u32[]{:S(2)}) %copy-start) | copy-done | bytes 2752536
  15.5 1.0 copy-done.1
  16.5 1.0 copy-done.2
  17.4 0.9 copy-done.3
  18.4 0.9 copy-done.4
  19.3 0.7 copy-done.5
  19.9 9.3 %cell_solve.1 = f32[128,6]{1,0:T(8,128)S(1)} custom-call(s32[128]{0:T(128)S(1)} %bitcast.33, s32[1]{0:T(128)} %bitcast.27.count_ref, f32[8,7,16,4096]{3,2,1,0:T(8,128)} %bitcast.34, f32[128,6]{1,0:T(8,128)S(1)} %bitcast.29, f32[128,6]{1,0:T(8,128)S(1)} %bitcast.32, f32[3,128,256]{2,1,0:T(8,128)S(1)} %broadcast_bitcast_fusion.maps_ref, ...), custom_call_target="tpu_custom_call" | custom-call | tf_op jit(solution)/shard_map/cell_solve/pallas_call | solution.py:285
  29.2 0.1 copy.19
  29.4 0.1 add_multiply_fusion.1
  29.5 0.1 fusion.17
  29.6 0.1 pad_add_fusion.8
  29.7 2.5 %collective-permute-start.2 = (f32[3,3,1,16]{3,2,1,0:T(1,128)S(1)}, f32[3,3,1,16]{3,2,1,0:T(1,128)S(1)}, u32[]{:S(2)}, u32[]{:S(2)}) collective-permute-start(f32[3,3,1,16]{3,2,1,0:T(1,128)S(1)} %pad_add_fusion.8), channel_id=1, source_target_pairs={{0,1},{1,2},{2,3},{3,4},{4,5},{5,6},{6,7},{7,8},{8,9},{9,10},{10,1... | collective-permute-start | bytes 1736 | tf_op jit(solution)/shard_map/ppermute | solution.py:325
  32.2 0.1 pad_add_fusion.2
  32.3 109.1 %collective-permute-done.2 = f32[3,3,1,16]{3,2,1,0:T(1,128)S(1)} collective-permute-done((f32[3,3,1,16]{3,2,1,0:T(1,128)S(1)}, f32[3,3,1,16]{3,2,1,0:T(1,128)S(1)}, u32[]{:S(2)}, u32[]{:S(2)}) %collective-permute-start.2) | collective-permute-done | bytes 608 | tf_op jit(solution)/shard_map/ppermute | solution.py:325
  141.5 0.1 add_add_fusion
  141.6 1.3 collective-permute-start.3
  142.9 0.7 copy.20
  143.6 1.0 collective-permute-done.3
  144.6 0.6 fusion.4
  (30 shorter events, 0.4 us)
Async XLA Ops:
  0.6 28.7 %copy-start.6 = (pred[3]{0:T(512)(128)(4,1)S(1)}, pred[3]{0:T(512)(128)(4,1)}, u32[]{:S(2)}) copy-start(pred[3]{0:T(512)(128)(4,1)} %constant.35.clone.1) | copy-start | bytes 13
  1.3 5.2 %collective-permute-start = (f32[3,1,4,16]{3,2,1,0:T(4,128)S(1)}, f32[3,1,4,16]{3,2,1,0:T(4,128)S(1)}, u32[]{:S(2)}, u32[]{:S(2)}) collective-permute-start(f32[3,1,4,16]{3,2,1,0:T(4,128)S(1)} %slice.110), channel_id=1, source_target_pairs={{16,0},{17,1},{18,2},{19,3},{20,4},{21,5},{22,6},{23,7},{24,8},{25... | collective-permute-start | bytes 2312 | tf_op jit(solution)/shard_map/ppermute | solution.py:325
  6.5 5.7 %collective-permute-start.1 = (f32[3,3,1,16]{3,2,1,0:T(1,128)S(1)}, f32[3,3,1,16]{3,2,1,0:T(1,128)S(1)}, u32[]{:S(2)}, u32[]{:S(2)}) collective-permute-start(f32[3,3,1,16]{3,2,1,0:T(1,128)S(1)} %slice.145), channel_id=1, source_target_pairs={{1,0},{2,1},{3,2},{4,3},{5,4},{6,5},{7,6},{8,7},{9,8},{10,9},{11,1... | collective-permute-start | bytes 1736 | tf_op jit(solution)/shard_map/ppermute | solution.py:325
  13.7 1.8 %copy-start = (f32[21,128,256]{2,1,0:T(8,128)S(1)}, f32[21,128,256]{2,1,0:T(8,128)}, u32[]{:S(2)}) copy-start(f32[21,128,256]{2,1,0:T(8,128)} %constant.41.clone.green_ref) | copy-start | bytes 8257540
  15.5 1.0 copy-start.1
  16.5 1.0 copy-start.2
  17.4 0.9 copy-start.3
  18.4 0.9 copy-start.4
  19.3 0.7 copy-start.5
  29.7 111.7 %collective-permute-start.2 = (f32[3,3,1,16]{3,2,1,0:T(1,128)S(1)}, f32[3,3,1,16]{3,2,1,0:T(1,128)S(1)}, u32[]{:S(2)}, u32[]{:S(2)}) collective-permute-start(f32[3,3,1,16]{3,2,1,0:T(1,128)S(1)} %pad_add_fusion.8), channel_id=1, source_target_pairs={{0,1},{1,2},{2,3},{3,4},{4,5},{5,6},{6,7},{7,8},{8,9},{9,10},{10,1... | collective-permute-start | bytes 1736 | tf_op jit(solution)/shard_map/ppermute | solution.py:325
  141.6 3.1 %collective-permute-start.3 = (f32[3,1,4,16]{3,2,1,0:T(4,128)S(1)}, f32[3,1,4,16]{3,2,1,0:T(4,128)S(1)}, u32[]{:S(2)}, u32[]{:S(2)}) collective-permute-start(f32[3,1,4,16]{3,2,1,0:T(4,128)S(1)} %fusion.10), channel_id=1, source_target_pairs={{0,16},{1,17},{2,18},{3,19},{4,20},{5,21},{6,22},{7,23},{8,24},{9,... | collective-permute-start | bytes 2312 | tf_op jit(solution)/shard_map/ppermute | solution.py:325
